TPU v7x, 32 devices: a whole 2x2x4 slice. The times are simulated.
32 devices in a mesh: dp: 2 (over x), blk: 8 (over z, core), uly: 2 (over y).
Axes of the slice: x: 2, y: 2, z: 4, core: 2. Of those that a mesh axis runs over, the one named last changes fastest.
Arguments:
- queries: bfloat16 [4096, 4096], P(('dp', 'blk', 'uly')), parts along dimension 0, may hold values from -24 to 24
- keys: bfloat16 [4096, 1024], P(('dp', 'blk', 'uly')), parts along dimension 0, may hold values from -12 to 12
- values: bfloat16 [4096, 1024], P(('dp', 'blk', 'uly')), parts along dimension 0, may hold values from -6 to 6
- doc_lengths: int32 [10], P('dp'), parts along dimension 0, may hold values from 1 to 512, 2048 in all
Outputs:
- attended: bfloat16 [4096, 4096], P(('dp', 'blk', 'uly')), parts along dimension 0
There are 2 independent parts, one for each index of `dp`. A program takes and returns all parts, laid end to end along the dimension named above; each array names one. Nothing has to cross between parts.
Inputs may be any that keep to these rules, and one draw needn't show every extreme that they name: `doc_lengths`: the 5 lengths sum to 2048; the longest is exactly 512.
All inputs are finite; a program needn't handle non-finite values.
Results may differ from a plain program's by a relative error of at most 0.0055.
Values may be sent and summed in bfloat16 or wider, within the bound.
A program may use at most 64 MiB of HBM per device.

v0:
```python
import math

import jax
import jax.numpy as jnp
from jax import lax
from jax.sharding import PartitionSpec as P

QUERY_HEADS = 32
KEY_VALUE_HEADS = 8
HEAD_SIZE = 128
CYCLE = 2


NEG_FILL = -1e30


def passed_along(block, axis, distance):
    devices = range(lax.axis_size(axis))
    route = [(i - distance, i) for i in devices if i - distance in devices]
    return lax.ppermute(block, axis, route)


def doc_index(positions, doc_lengths):
    ends = jnp.cumsum(doc_lengths)
    return jnp.sum((positions[:, None] >= ends[None, :]).astype(jnp.int32), axis=1)


def per_device(queries, keys, values, doc_lengths):
    token_rows = queries.shape[0]
    q_heads = queries.reshape(token_rows, QUERY_HEADS, HEAD_SIZE)
    kv_heads = jnp.stack(
        [
            keys.reshape(token_rows, KEY_VALUE_HEADS, HEAD_SIZE),
            values.reshape(token_rows, KEY_VALUE_HEADS, HEAD_SIZE),
        ],
        axis=2,
    )
    q_local, kv_local = (
        lax.all_to_all(q_heads, "uly", split_axis=1, concat_axis=0, tiled=True),
        lax.all_to_all(kv_heads, "uly", split_axis=1, concat_axis=0, tiled=True),
    )
    block = q_local.shape[0]
    groups = kv_local.shape[1]
    group_repeat = QUERY_HEADS // KEY_VALUE_HEADS
    sub_rows = min(block, 512)
    pieces = block // sub_rows
    position = lax.axis_index("blk")
    rows = jnp.arange(block, dtype=jnp.int32)
    q_pos = position * block + rows
    q_doc = doc_index(q_pos, doc_lengths)
    q_parts = q_local.reshape(pieces, sub_rows, groups, group_repeat, HEAD_SIZE)
    pos_parts = q_pos.reshape(pieces, sub_rows)
    doc_parts = q_doc.reshape(pieces, sub_rows)
    scale = 1.0 / math.sqrt(HEAD_SIZE)

    def attend(state, kv_piece, back):
        k_pos = (position - back) * block + rows
        k_doc = doc_index(k_pos, doc_lengths)
        key_part = kv_piece[:, :, 0, :]
        value_part = kv_piece[:, :, 1, :]

        def one_part(items):
            q_part, pos_part, doc_part, peak, total, summed = items
            allowed = (
                (k_pos[None, :] <= pos_part[:, None])
                & (k_pos[None, :] >= 0)
                & (k_doc[None, :] == doc_part[:, None])
            )
            scores = (
                jnp.einsum("qgrd,kgd->qgrk", q_part, key_part, preferred_element_type=jnp.float32)
                * scale
            )
            scores = jnp.where(allowed[:, None, None, :], scores, NEG_FILL)
            new_peak = jnp.maximum(peak, jnp.max(scores, axis=-1))
            weights = jnp.where(
                allowed[:, None, None, :], jnp.exp(scores - new_peak[..., None]), 0.0
            )
            factor = jnp.exp(peak - new_peak)
            new_total = total * factor + jnp.sum(weights, axis=-1)
            update = jnp.einsum(
                "qgrk,kgd->qgrd",
                weights.astype(jnp.bfloat16),
                value_part,
                preferred_element_type=jnp.float32,
            )
            return (new_peak, new_total, summed * factor[..., None] + update)

        peak, total, summed = state
        return lax.map(one_part, (q_parts, pos_parts, doc_parts, peak, total, summed))

    start_state = (
        jnp.full((pieces, sub_rows, groups, group_repeat), NEG_FILL, jnp.float32),
        jnp.zeros((pieces, sub_rows, groups, group_repeat), jnp.float32),
        jnp.zeros((pieces, sub_rows, groups, group_repeat, HEAD_SIZE), jnp.float32),
    )
    state = attend(start_state, kv_local, 0)
    moving = kv_local
    for back in range(1, CYCLE + 1):
        moving = passed_along(moving, "blk", 1)
        state = attend(state, moving, back)
    peak, total, summed = state
    result = (
        (summed / total[..., None])
        .astype(jnp.bfloat16)
        .reshape(block, groups * group_repeat, HEAD_SIZE)
    )
    returned = lax.all_to_all(result, "uly", split_axis=0, concat_axis=1, tiled=True)
    return returned.reshape(token_rows, QUERY_HEADS * HEAD_SIZE)


def solution(mesh):
    in_specs = (
        P(("dp", "blk", "uly"), None),
        P(("dp", "blk", "uly"), None),
        P(("dp", "blk", "uly"), None),
        P("dp"),
    )
    out_specs = P(("dp", "blk", "uly"), None)
    return jax.shard_map(
        per_device, mesh=mesh, in_specs=in_specs, out_specs=out_specs, check_vma=False
    )
```

profile of v0, /device:TPU:8, one launch (start us, length us, event | category | flops | bytes accessed | tf_op | source)
XLA Modules:
  0.0 68.5 jit_solution(12561544789993422418)
XLA Ops:
  0.0 0.0 copy-start
  0.0 0.0 copy-start.1
  0.0 1.2 %copy.65 = bf16[128,1024]{0,1:T(8,128)(2,1)S(1)} copy(bf16[128,1024]{1,0:T(8,128)(2,1)} %param.5) | data formatting | bytes 524288 | tf_op args[1]
  1.2 1.1 %copy.66 = bf16[128,1024]{0,1:T(8,128)(2,1)S(1)} copy(bf16[128,1024]{1,0:T(8,128)(2,1)} %param.6) | data formatting | bytes 524288 | tf_op args[2]
  2.3 0.1 pad_maximum_fusion
  2.4 0.8 %copy.67 = bf16[128,8,2,128]{0,3,2,1:T(8,128)(2,1)} copy(bf16[128,8,2,128]{0,3,1,2:T(8,128)(2,1)S(1)} %pad_maximum_fusion) | data formatting | bytes 1048576 | tf_op jit(solution)/shard_map/stack | solution.py:31
  3.2 3.5 %all-to-all-start = ((bf16[128,8,2,128]{0,3,2,1:T(8,128)(2,1)}), bf16[128,8,2,128]{0,3,2,1:T(8,128)(2,1)S(1)}, u32[]{:S(2)}, u32[]{:S(2)}) async-start(bf16[128,8,2,128]{0,3,2,1:T(8,128)(2,1)} %copy.67), calls=%async_computation | async-start | bytes 1048576 | tf_op jit(solution)/shard_map/all_to_all | solution.py:40
  6.7 0.0 copy-done
  6.7 0.7 copy.70
  7.4 1.3 %copy.71 = bf16[128,32,128]{2,0,1:T(8,128)(2,1)} copy(bf16[128,32,128]{0,2,1:T(8,128)(2,1)S(1)} %bitcast.129) | data formatting | bytes 2097152 | tf_op jit(solution)/shard_map/reshape | solution.py:30
  8.7 0.0 copy-done.1
  8.7 0.2 reduce-window.8
  8.9 6.0 %all-to-all-done = bf16[128,8,2,128]{0,3,2,1:T(8,128)(2,1)S(1)} async-done(((bf16[128,8,2,128]{0,3,2,1:T(8,128)(2,1)}), bf16[128,8,2,128]{0,3,2,1:T(8,128)(2,1)S(1)}, u32[]{:S(2)}, u32[]{:S(2)}) %all-to-all-start) | async-done | bytes 524320 | tf_op jit(solution)/shard_map/all_to_all | solution.py:40
  15.0 3.6 %all-to-all-start.1 = ((bf16[128,32,128]{2,0,1:T(8,128)(2,1)}), bf16[128,32,128]{2,0,1:T(8,128)(2,1)S(1)}, u32[]{:S(2)}, u32[]{:S(2)}) async-start(bf16[128,32,128]{2,0,1:T(8,128)(2,1)} %copy.71), calls=%async_computation.1 | async-start | bytes 2097152 | tf_op jit(solution)/shard_map/all_to_all | solution.py:39
  18.6 0.3 copy.69
  18.8 1.9 %collective-permute-start = (bf16[256,4,2,128]{3,0,1,2:T(8,128)(2,1)S(1)}, bf16[256,4,2,128]{3,0,1,2:T(8,128)(2,1)S(1)}, u32[]{:S(2)}, u32[]{:S(2)}) collective-permute-start(bf16[256,4,2,128]{3,0,1,2:T(8,128)(2,1)S(1)} %bitcast.131), channel_id=1, source_target_pairs={{0,2},{2,4},{4,6},{6,8},{8,10},{10,12},{12,14},{1,3},{3,5},{5,7},{... | collective-permute-start | bytes 1572872 | tf_op jit(solution)/shard_map/ppermute | solution.py:20
  20.8 0.1 convert_reduce_fusion
  20.9 0.5 compare_and_fusion.2
  21.4 10.1 %all-to-all-done.1 = bf16[128,32,128]{2,0,1:T(8,128)(2,1)S(1)} async-done(((bf16[128,32,128]{2,0,1:T(8,128)(2,1)}), bf16[128,32,128]{2,0,1:T(8,128)(2,1)S(1)}, u32[]{:S(2)}, u32[]{:S(2)}) %all-to-all-start.1) | async-done | bytes 1048608 | tf_op jit(solution)/shard_map/all_to_all | solution.py:39
  31.5 0.1 copy.73
  31.6 0.0 collective-permute-done
  31.7 1.9 %collective-permute-start.1 = (bf16[256,4,2,128]{3,0,1,2:T(8,128)(2,1)S(1)}, bf16[256,4,2,128]{3,0,1,2:T(8,128)(2,1)S(1)}, u32[]{:S(2)}, u32[]{:S(2)}) collective-permute-start(bf16[256,4,2,128]{3,0,1,2:T(8,128)(2,1)S(1)} %collective-permute-done), channel_id=1, source_target_pairs={{0,2},{2,4},{4,6},{6,8},{8,10},{10,12},{12,14},{1,3},{3,5},{5,7},{... | collective-permute-start | bytes 1572872 | tf_op jit(solution)/shard_map/ppermute | solution.py:20
  33.6 0.8 %fusion = (f32[256,4,4]{0,2,1:T(4,128)S(1)}, f32[4,256,256,4]{2,1,3,0:T(8,128)S(1)}) fusion(pred[256,256]{0,1:T(8,128)(4,1)S(1)} %get-tuple-element.101, bf16[256,4,4,128]{3,0,2,1:T(8,128)(2,1)S(1)} %bitcast.123, bf16[256,4,2,128]{3,0,1,2:T(8,128)(2,1)S(1)} %bitcast.132), kind=kOutput, calls=%fused_computation.6 | convolution fusion | flops 271577088 | bytes 5586944 | tf_op jit(solution)/shard_map/while/body/eval_jaxpr/qgrd,kgd->qgrk/dot_general | solution.py:70
  34.4 0.8 %fusion.1 = (f32[256,4,4]{0,2,1:T(4,128)S(1)}, f32[4,256,256,4]{2,1,3,0:T(8,128)S(1)}) fusion(pred[256,256]{0,1:T(8,128)(4,1)S(1)} %get-tuple-element.103, bf16[256,4,4,128]{3,0,2,1:T(8,128)(2,1)S(1)} %bitcast.124, bf16[256,4,2,128]{3,0,1,2:T(8,128)(2,1)S(1)} %collective-permute-done), kind=kOutput, calls=%fused_computation.7 | convolution fusion | flops 271577088 | bytes 5586944 | tf_op jit(solution)/shard_map/while/body/eval_jaxpr/qgrd,kgd->qgrk/dot_general | solution.py:70
  35.2 7.0 %collective-permute-done.1 = bf16[256,4,2,128]{3,0,1,2:T(8,128)(2,1)S(1)} collective-permute-done((bf16[256,4,2,128]{3,0,1,2:T(8,128)(2,1)S(1)}, bf16[256,4,2,128]{3,0,1,2:T(8,128)(2,1)S(1)}, u32[]{:S(2)}, u32[]{:S(2)}) %collective-permute-start.1) | collective-permute-done | bytes 524320 | tf_op jit(solution)/shard_map/ppermute | solution.py:20
  42.2 0.8 %fusion.2 = (f32[256,4,4]{0,2,1:T(4,128)S(1)}, f32[4,256,256,4]{2,1,3,0:T(8,128)S(1)}) fusion(pred[256,256]{0,1:T(8,128)(4,1)S(1)} %get-tuple-element.102, bf16[256,4,4,128]{3,0,2,1:T(8,128)(2,1)S(1)} %bitcast.125, bf16[256,4,2,128]{3,0,1,2:T(8,128)(2,1)S(1)} %collective-permute-done.1), kind=kOutput, calls=%fused_computation.8 | convolution fusion | flops 271577088 | bytes 5586944 | tf_op jit(solution)/shard_map/while/body/eval_jaxpr/qgrd,kgd->qgrk/dot_general | solution.py:70
  43.0 1.0 %fusion.3 = f32[256,4,4]{0,2,1:T(4,128)S(1)} fusion(f32[4,256,256,4]{2,1,3,0:T(8,128)S(1)} %get-tuple-element.109, f32[256,4,4]{0,2,1:T(4,128)S(1)} %get-tuple-element.100, pred[256,256]{0,1:T(8,128)(4,1)S(1)} %get-tuple-element.101), kind=kLoop, calls=%fused_computation.9 | loop fusion | flops 5238784 | bytes 4292608 | tf_op jit(solution)/shard_map/while/body/eval_jaxpr/reduce_sum | solution.py:79
  44.0 1.2 %fusion.13 = f32[4,128,256,4]{2,1,3,0:T(8,128)S(1)} fusion(f32[4,256,256,4]{2,1,3,0:T(8,128)S(1)} %get-tuple-element.109, f32[256,4,4]{0,2,1:T(4,128)S(1)} %get-tuple-element.100, pred[256,256]{0,1:T(8,128)(4,1)S(1)} %get-tuple-element.101, bf16[256,4,2,128]{3,0,1,2:T(8,128)(2,1)S(1)} %bitcast.133), kind=kOutput, calls=%fused_computation.17 | convolution fusion | flops 273678336 | bytes 6635520 | tf_op jit(solution)/shard_map/while/body/eval_jaxpr/qgrk,kgd->qgrd/dot_general | solution.py:80
  45.2 1.0 %fusion.7 = f32[256,4,4]{0,2,1:T(4,128)S(1)} fusion(f32[4,256,256,4]{2,1,3,0:T(8,128)S(1)} %get-tuple-element.105, f32[256,4,4]{0,2,1:T(4,128)S(1)} %get-tuple-element.83, pred[256,256]{0,1:T(8,128)(4,1)S(1)} %get-tuple-element.102), kind=kLoop, calls=%fused_computation.13 | loop fusion | flops 5238784 | bytes 4292608 | tf_op jit(solution)/shard_map/while/body/eval_jaxpr/reduce_sum | solution.py:79
  46.3 1.0 %fusion.5 = f32[256,4,4]{0,2,1:T(4,128)S(1)} fusion(f32[4,256,256,4]{2,1,3,0:T(8,128)S(1)} %get-tuple-element.107, f32[256,4,4]{0,2,1:T(4,128)S(1)} %get-tuple-element.84, pred[256,256]{0,1:T(8,128)(4,1)S(1)} %get-tuple-element.103), kind=kLoop, calls=%fused_computation.11 | loop fusion | flops 5238784 | bytes 4292608 | tf_op jit(solution)/shard_map/while/body/eval_jaxpr/reduce_sum | solution.py:79
  47.3 1.2 %fusion.11 = f32[4,128,256,4]{2,1,3,0:T(8,128)S(1)} fusion(f32[4,256,256,4]{2,1,3,0:T(8,128)S(1)} %get-tuple-element.107, f32[256,4,4]{0,2,1:T(4,128)S(1)} %get-tuple-element.84, pred[256,256]{0,1:T(8,128)(4,1)S(1)} %get-tuple-element.103, bf16[256,4,2,128]{3,0,1,2:T(8,128)(2,1)S(1)} %collective-permute-done), kind=kOutput, calls=%fused_computation.16 | convolution fusion | flops 273678336 | bytes 6635520 | tf_op jit(solution)/shard_map/while/body/eval_jaxpr/qgrk,kgd->qgrd/dot_general | solution.py:80
  48.6 1.5 %fusion.16 = bf16[256,4,4,128]{0,3,2,1:T(8,128)(2,1)S(1)} fusion(f32[4,128,256,4]{2,1,3,0:T(8,128)S(1)} %fusion.11, f32[4,128,256,4]{2,1,3,0:T(8,128)S(1)} %fusion.13, f32[256,4,4]{0,2,1:T(4,128)S(1)} %get-tuple-element.80, f32[256,4,4]{0,2,1:T(4,128)S(1)} %get-tuple-element.82, f32[256,4,4]{0,2,1:T(4,128)S(1)} %get-tuple-element.81, ...), kind=kOutput, calls=%fused_computation.20 | convolution fusion | flops 277348352 | bytes 9846784 | tf_op jit(solution)/shard_map/while/body/eval_jaxpr/qgrk,kgd->qgrd/dot_general | solution.py:80
  50.1 1.1 %copy.80 = bf16[256,16,128]{2,1,0:T(8,128)(2,1)S(1)} copy(bf16[256,16,128]{0,2,1:T(8,128)(2,1)S(1)} %bitcast.134) | data formatting | bytes 2097152 | tf_op jit(solution)/shard_map/reshape | solution.py:105
  51.2 15.7 %all_to_all.48 = bf16[256,16,128]{2,1,0:T(8,128)(2,1)S(1)} all-to-all(bf16[256,16,128]{2,1,0:T(8,128)(2,1)S(1)} %copy.80), channel_id=1, replica_groups=mesh['dp'=2,'blk'=8,'uly'=2] {'uly'}, dimensions={0} | all-to-all | bytes 2097152 | tf_op jit(solution)/shard_map/all_to_all | solution.py:107
  66.9 0.2 copy.81
  67.1 1.4 %copy.101 = bf16[16,8,32,128]{3,1,2,0:T(8,128)(2,1)} copy(bf16[16,8,32,128]{3,2,1,0:T(8,128)(2,1)S(1)} %bitcast.128) | data formatting | bytes 2097152
  (6 shorter events, 0.1 us)
Async XLA Ops:
  0.0 6.7 %copy-start = (bf16[128,4096]{1,0:T(8,128)(2,1)S(1)}, bf16[128,4096]{1,0:T(8,128)(2,1)}, u32[]{:S(2)}) copy-start(bf16[128,4096]{1,0:T(8,128)(2,1)} %param.4) | copy-start | bytes 3145732
  0.0 8.7 %copy-start.1 = (s32[5]{0:T(128)S(1)}, s32[5]{0:T(128)}, u32[]{:S(2)}) copy-start(s32[5]{0:T(128)} %param.7) | copy-start | bytes 64
  3.2 11.7 %all-to-all-start = ((bf16[128,8,2,128]{0,3,2,1:T(8,128)(2,1)}), bf16[128,8,2,128]{0,3,2,1:T(8,128)(2,1)S(1)}, u32[]{:S(2)}, u32[]{:S(2)}) async-start(bf16[128,8,2,128]{0,3,2,1:T(8,128)(2,1)} %copy.67), calls=%async_computation | async-start | bytes 1048576 | tf_op jit(solution)/shard_map/all_to_all | solution.py:40
  15.0 16.6 %all-to-all-start.1 = ((bf16[128,32,128]{2,0,1:T(8,128)(2,1)}), bf16[128,32,128]{2,0,1:T(8,128)(2,1)S(1)}, u32[]{:S(2)}, u32[]{:S(2)}) async-start(bf16[128,32,128]{2,0,1:T(8,128)(2,1)} %copy.71), calls=%async_computation.1 | async-start | bytes 2097152 | tf_op jit(solution)/shard_map/all_to_all | solution.py:39
  18.8 12.8 %collective-permute-start = (bf16[256,4,2,128]{3,0,1,2:T(8,128)(2,1)S(1)}, bf16[256,4,2,128]{3,0,1,2:T(8,128)(2,1)S(1)}, u32[]{:S(2)}, u32[]{:S(2)}) collective-permute-start(bf16[256,4,2,128]{3,0,1,2:T(8,128)(2,1)S(1)} %bitcast.131), channel_id=1, source_target_pairs={{0,2},{2,4},{4,6},{6,8},{8,10},{10,12},{12,14},{1,3},{3,5},{5,7},{... | collective-permute-start | bytes 1572872 | tf_op jit(solution)/shard_map/ppermute | solution.py:20
  31.7 10.5 %collective-permute-start.1 = (bf16[256,4,2,128]{3,0,1,2:T(8,128)(2,1)S(1)}, bf16[256,4,2,128]{3,0,1,2:T(8,128)(2,1)S(1)}, u32[]{:S(2)}, u32[]{:S(2)}) collective-permute-start(bf16[256,4,2,128]{3,0,1,2:T(8,128)(2,1)S(1)} %collective-permute-done), channel_id=1, source_target_pairs={{0,2},{2,4},{4,6},{6,8},{8,10},{10,12},{12,14},{1,3},{3,5},{5,7},{... | collective-permute-start | bytes 1572872 | tf_op jit(solution)/shard_map/ppermute | solution.py:20
where the time goes:
time: 68.9 us; the launch traced here: 68.5 us
  waiting for transfers between devices  23.1 us (34%)
  blocking collectives  15.7 us (23%)
  starting transfers between devices  10.9 us (16%)
  local copies, waits for them, and re-layouts  8.18 us (12%)
  matrix products  6.28 us (9%)
  other arithmetic  4.07 us (6%)
    all_to_all x1, blocking collectives, per_device(): lax.all_to_all(result, 'uly', split_axis=0, concat_axis=1, tiled=True)  15.7 us
    all_to_all x1, waiting for transfers between devices, per_device(): lax.all_to_all(q_heads, 'uly', split_axis=1, concat_axis=0, tiled=True)  10.1 us
    ppermute x2, waiting for transfers between devices, passed_along(): return lax.ppermute(block, axis, route)  7 us
    all_to_all x1, waiting for transfers between devices, per_device(): lax.all_to_all(kv_heads, 'uly', split_axis=1, concat_axis=0, tiled=True)  6.04 us
    unnamed x8, local copies, waits for them, and re-layouts  4.41 us
    dot_general x3, matrix products, one_part(): jnp.einsum('qgrk,kgd->qgrd', weights.astype(jnp.bfloat16), value_part, pr...  3.93 us
    ppermute x2, starting transfers between devices, passed_along(): return lax.ppermute(block, axis, route)  3.84 us
    all_to_all x1, starting transfers between devices, per_device(): lax.all_to_all(q_heads, 'uly', split_axis=1, concat_axis=0, tiled=True)  3.58 us
  transfers between devices with their start and end apart: 4, of which 3 were waited for; matrix products, arithmetic and copies ran while one was open for 7% of the time, Pallas kernels for 0%

commit v1 on v0

v1 whole, which is shorter than its diff:
```python
import functools
import math

import jax
import jax.numpy as jnp
from jax import lax
from jax.experimental import pallas as pl
from jax.experimental.pallas import tpu as pltpu
from jax.sharding import PartitionSpec as P

QUERY_HEADS = 32
KEY_VALUE_HEADS = 8
HEAD_SIZE = 128
CYCLE = 2
GROUP = QUERY_HEADS // KEY_VALUE_HEADS

NEG_FILL = -1e30
AHEAD = 3
ORDER_FOUR = (4, 1, 2, 3)

FOUR = (
    ((0, 4, None), (0, 1, None), (0, 2, None)),
    ((0, 4, None), (0, 1, None), (0, 2, None), (1, 2, None), (4, -1, 1)),
    ((0, 4, None), (0, 1, None), (1, 2, 0), (4, -2, None), (4, -1, 1), (3, -2, None)),
    ((0, 4, None), (1, 2, 0), (4, -1, None), (4, -2, None)),
)


def routes_for(uly, blocks):
    if CYCLE * uly == 4 and blocks % 4 == 0:
        return FOUR, ORDER_FOUR
    reach = CYCLE * uly
    direct = tuple((0, k, None) for k in range(1, reach + 1))
    return (direct,), tuple(range(1, reach + 1))


def kernel(
    uly, blocks, q_hbm, k_hbm, v_hbm, len_ref, out_hbm,
    q_ref, kv_ref, o_ref, bias_ref, load_sem, q_sem, out_sem, send_sem, recv_sem,
):
    rows = q_ref.shape[0]
    reach = CYCLE * uly
    routes, order = routes_for(uly, blocks)
    period = len(routes)
    b = lax.axis_index("blk") * uly + lax.axis_index("uly")
    role = lax.rem(b, period)

    def target(other):
        return {"blk": other // uly, "uly": lax.rem(other, uly)}

    def place(g, slot):
        return kv_ref.at[g, :, pl.ds((reach - slot) * rows, rows), :]

    def loads(g):
        cols = pl.ds(pl.multiple_of(g * HEAD_SIZE, HEAD_SIZE), HEAD_SIZE)
        here = pl.ds(reach * rows, rows)
        return [
            pltpu.make_async_copy(src.at[:, cols], kv_ref.at[g, i, here, :], load_sem.at[i, g])
            for i, src in enumerate((k_hbm, v_hbm))
        ]

    q_copy = pltpu.make_async_copy(q_hbm, q_ref, q_sem)

    @pl.loop(0, KEY_VALUE_HEADS)
    def _(g):
        for copy in loads(g):
            copy.start()

    q_copy.start()

    spans = sorted({abs(delta) for role_routes in routes for _, delta, _ in role_routes})
    barrier = pltpu.get_barrier_semaphore()
    expected = 0
    for span in spans:
        for other in (b + span, b - span):
            valid = (other >= 0) & (other < blocks)
            expected = expected + valid.astype(jnp.int32)

            @pl.when(valid)
            def _():
                pl.semaphore_signal(
                    barrier, inc=1, device_id=target(other), device_id_type=pl.DeviceIdType.MESH
                )

    for slot in range(1, reach + 1):

        @pl.when(b < slot)
        def _():
            @pl.loop(0, KEY_VALUE_HEADS)
            def _(g):
                kv_ref[g, :, pl.ds((reach - slot) * rows, rows), :] = jnp.zeros(
                    (2, rows, HEAD_SIZE), kv_ref.dtype
                )

    q_pos = b * rows + lax.broadcasted_iota(jnp.int32, (rows, 1), 0)
    first = jnp.zeros((rows, 1), jnp.int32)
    end = jnp.int32(0)
    for d in range(len_ref.shape[0]):
        end = end + len_ref[d]
        first = jnp.where(q_pos >= end, end, first)
    k_pos = (b - reach) * rows + lax.broadcasted_iota(jnp.int32, bias_ref.shape, 1)
    bias_ref[...] = jnp.where((k_pos <= q_pos) & (k_pos >= first), 0.0, NEG_FILL)

    pl.semaphore_wait(barrier, expected)

    def each_route(g, only, act):
        for r, role_routes in enumerate(routes):
            for n, (slot, delta, parity) in enumerate(role_routes):
                if slot not in only:
                    continue
                other = b + delta
                go = (role == r) & (b >= slot) & (other >= 0) & (other < blocks)
                if parity is not None:
                    go = go & (lax.rem(g, 2) == parity)

                @pl.when(go)
                def _():
                    act(
                        pltpu.make_async_remote_copy(
                            src_ref=place(g, slot),
                            dst_ref=place(g, slot + delta),
                            send_sem=send_sem.at[n, g],
                            recv_sem=recv_sem.at[slot + delta - 1, g],
                            device_id=target(other),
                            device_id_type=pl.DeviceIdType.MESH,
                        )
                    )

    def send_own(g):
        for copy in loads(g):
            copy.wait()
        each_route(g, (0,), lambda copy: copy.start())

    @pl.loop(0, AHEAD)
    def _(g):
        send_own(g)

    q_copy.wait()
    factor = math.log2(math.e) / math.sqrt(HEAD_SIZE)

    def out_copy(g):
        width = GROUP * HEAD_SIZE
        cols = pl.ds(pl.multiple_of(g * width, width), width)
        return pltpu.make_async_copy(o_ref.at[:, cols], out_hbm.at[:, cols], out_sem.at[g])

    @pl.loop(0, KEY_VALUE_HEADS)
    def _(g):
        @pl.when(g + AHEAD < KEY_VALUE_HEADS)
        def _():
            send_own(g + AHEAD)

        for slot in order:

            @pl.when(b >= slot)
            def _():
                pltpu.make_async_copy(
                    place(g, slot), place(g, slot), recv_sem.at[slot - 1, g]
                ).wait()

            each_route(g, (slot,), lambda copy: copy.start())

        keys = kv_ref[g, 0]
        values = kv_ref[g, 1]

        def cols(r):
            return pl.ds(pl.multiple_of((g * GROUP + r) * HEAD_SIZE, HEAD_SIZE), HEAD_SIZE)

        queries = jnp.concatenate([q_ref[:, cols(r)] for r in range(GROUP)], axis=0)
        scores = lax.dot_general(
            queries, keys, (((1,), (1,)), ((), ())), preferred_element_type=jnp.float32
        )
        parts, totals = [], []
        for r in range(GROUP):
            part = scores[r * rows:(r + 1) * rows] + bias_ref[...]
            peak = jnp.max(part, axis=1, keepdims=True)
            weights = jnp.exp2((part - peak) * factor)
            totals.append(jnp.sum(weights, axis=1, keepdims=True))
            parts.append(weights.astype(jnp.bfloat16))
        summed = jnp.dot(
            jnp.concatenate(parts, axis=0), values, preferred_element_type=jnp.float32
        )
        for r in range(GROUP):
            o_ref[:, cols(r)] = (summed[r * rows:(r + 1) * rows] / totals[r]).astype(o_ref.dtype)
        out_copy(g).start()

    @pl.loop(0, KEY_VALUE_HEADS)
    def _(g):
        each_route(g, tuple(range(reach + 1)), lambda copy: copy.wait_send())
        out_copy(g).wait()


def per_device(uly, blocks, queries, keys, values, doc_lengths):
    rows = queries.shape[0]
    reach = CYCLE * uly
    routes, _ = routes_for(uly, blocks)
    most = max(len(role_routes) for role_routes in routes)
    span = (reach + 1) * rows
    flops = 4 * rows * span * QUERY_HEADS * HEAD_SIZE
    any_space = pl.BlockSpec(memory_space=pl.ANY)
    return pl.pallas_call(
        functools.partial(kernel, uly, blocks),
        out_shape=jax.ShapeDtypeStruct(queries.shape, queries.dtype),
        in_specs=[any_space, any_space, any_space, pl.BlockSpec(memory_space=pltpu.SMEM)],
        out_specs=any_space,
        scratch_shapes=[
            pltpu.VMEM(queries.shape, queries.dtype),
            pltpu.VMEM((KEY_VALUE_HEADS, 2, span, HEAD_SIZE), keys.dtype),
            pltpu.VMEM(queries.shape, queries.dtype),
            pltpu.VMEM((rows, span), jnp.float32),
            pltpu.SemaphoreType.DMA((2, KEY_VALUE_HEADS)),
            pltpu.SemaphoreType.DMA,
            pltpu.SemaphoreType.DMA((KEY_VALUE_HEADS,)),
            pltpu.SemaphoreType.DMA((most, KEY_VALUE_HEADS)),
            pltpu.SemaphoreType.DMA((reach, KEY_VALUE_HEADS)),
        ],
        cost_estimate=pl.CostEstimate(
            flops=flops,
            bytes_accessed=2 * (queries.size * 2 + keys.size * 2),
            transcendentals=rows * span * QUERY_HEADS,
        ),
        compiler_params=pltpu.CompilerParams(
            collective_id=0, has_side_effects=True, vmem_limit_bytes=48 * 1024 * 1024
        ),
    )(queries, keys, values, doc_lengths)


def solution(mesh):
    in_specs = (
        P(("dp", "blk", "uly"), None),
        P(("dp", "blk", "uly"), None),
        P(("dp", "blk", "uly"), None),
        P("dp"),
    )
    out_specs = P(("dp", "blk", "uly"), None)
    uly = mesh.shape["uly"]
    blocks = mesh.shape["blk"] * uly
    return jax.shard_map(
        functools.partial(per_device, uly, blocks),
        mesh=mesh, in_specs=in_specs, out_specs=out_specs, check_vma=False,
    )
```

time: 68.9 us -> 42 us (0.61)
  the two profiles are of different devices: /device:TPU:8 before, /device:TPU:16 now
where the time goes in v1:
time: 42 us; the launch traced here: 41.8 us
  Pallas kernels  37 us (88%)
  local copies, waits for them, and re-layouts  4.75 us (11%)
    pallas_call x1, Pallas kernels, per_device(): pl.pallas_call(functools.partial(kernel, uly, blocks), out_shape=jax.Shap...  37 us
    unnamed x9, local copies, waits for them, and re-layouts  4.75 us

profile of v1, /device:TPU:16, one launch (start us, length us, event | category | flops | bytes accessed | tf_op | source)
XLA Modules:
  0.0 41.8 jit_solution(4797339946640059971)
XLA Ops:
  0.0 0.0 copy-start
  0.0 1.2 %copy-done = bf16[128,4096]{1,0:T(8,128)(2,1)S(1)} copy-done((bf16[128,4096]{1,0:T(8,128)(2,1)S(1)}, bf16[128,4096]{1,0:T(8,128)(2,1)}, u32[]{:S(2)}) %copy-start) | copy-done | bytes 1048600
  1.2 0.0 copy-start.1
  1.2 0.9 %copy-done.1 = bf16[128,1024]{1,0:T(8,128)(2,1)S(1)} copy-done((bf16[128,1024]{1,0:T(8,128)(2,1)S(1)}, bf16[128,1024]{1,0:T(8,128)(2,1)}, u32[]{:S(2)}) %copy-start.1) | copy-done | bytes 262168
  2.2 0.0 copy-start.2
  2.2 0.9 %copy-done.2 = bf16[128,1024]{1,0:T(8,128)(2,1)S(1)} copy-done((bf16[128,1024]{1,0:T(8,128)(2,1)S(1)}, bf16[128,1024]{1,0:T(8,128)(2,1)}, u32[]{:S(2)}) %copy-start.2) | copy-done | bytes 262168
  3.1 0.0 copy-start.3
  3.1 0.7 %copy-done.3 = s32[5]{0:T(128)S(1)} copy-done((s32[5]{0:T(128)S(1)}, s32[5]{0:T(128)}, u32[]{:S(2)}) %copy-start.3) | copy-done | bytes 44
  3.8 37.0 %shard_map.46 = bf16[128,4096]{1,0:T(8,128)(2,1)S(1)} custom-call(bf16[128,4096]{1,0:T(8,128)(2,1)S(1)} %copy-done, bf16[128,1024]{1,0:T(8,128)(2,1)S(1)} %copy-done.1, bf16[128,1024]{1,0:T(8,128)(2,1)S(1)} %copy-done.2, s32[5]{0:T(128)S(1)} %copy-done.3), custom_call_target="tpu_custom_call" | custom-call | flops 1342177280 | bytes 2621440 | tf_op jit(solution)/shard_map/pallas_call | solution.py:200
  40.8 1.0 %copy.6 = bf16[128,4096]{1,0:T(8,128)(2,1)} copy(bf16[128,4096]{1,0:T(8,128)(2,1)S(1)} %shard_map.46) | data formatting | bytes 2097152
Async XLA Ops:
  0.0 1.2 %copy-start = (bf16[128,4096]{1,0:T(8,128)(2,1)S(1)}, bf16[128,4096]{1,0:T(8,128)(2,1)}, u32[]{:S(2)}) copy-start(bf16[128,4096]{1,0:T(8,128)(2,1)} %q_hbm.1) | copy-start | bytes 3145732
  1.2 0.9 %copy-start.1 = (bf16[128,1024]{1,0:T(8,128)(2,1)S(1)}, bf16[128,1024]{1,0:T(8,128)(2,1)}, u32[]{:S(2)}) copy-start(bf16[128,1024]{1,0:T(8,128)(2,1)} %k_hbm.1) | copy-start | bytes 786436
  2.2 0.9 %copy-start.2 = (bf16[128,1024]{1,0:T(8,128)(2,1)S(1)}, bf16[128,1024]{1,0:T(8,128)(2,1)}, u32[]{:S(2)}) copy-start(bf16[128,1024]{1,0:T(8,128)(2,1)} %v_hbm.1) | copy-start | bytes 786436
  3.1 0.7 %copy-start.3 = (s32[5]{0:T(128)S(1)}, s32[5]{0:T(128)}, u32[]{:S(2)}) copy-start(s32[5]{0:T(128)} %len_ref.1) | copy-start | bytes 64

commit v2 on v1

--- a/solution.py
+++ b/solution.py
@@ -16,7 +16,6 @@
 
 NEG_FILL = -1e30
 AHEAD = 3
-ORDER_FOUR = (4, 1, 2, 3)
 
 FOUR = (
     ((0, 4, None), (0, 1, None), (0, 2, None)),
@@ -24,23 +23,30 @@
     ((0, 4, None), (0, 1, None), (1, 2, 0), (4, -2, None), (4, -1, 1), (3, -2, None)),
     ((0, 4, None), (1, 2, 0), (4, -1, None), (4, -2, None)),
 )
+FOUR_HOPS = (
+    ((4,), (2, 3), (1,)),
+    ((4, 1), (2, 3), ()),
+    ((4, 1, 2), (3,), ()),
+    ((4, 1, 2), (3,), ()),
+)
 
 
 def routes_for(uly, blocks):
     if CYCLE * uly == 4 and blocks % 4 == 0:
-        return FOUR, ORDER_FOUR
+        return FOUR, FOUR_HOPS
     reach = CYCLE * uly
     direct = tuple((0, k, None) for k in range(1, reach + 1))
-    return (direct,), tuple(range(1, reach + 1))
+    return (direct,), ((tuple(range(1, reach + 1)),),)
 
 
 def kernel(
-    uly, blocks, q_hbm, k_hbm, v_hbm, len_ref, out_hbm,
-    q_ref, kv_ref, o_ref, bias_ref, load_sem, q_sem, out_sem, send_sem, recv_sem,
+    uly, blocks, q_hbm, k_hbm, v_hbm, len_hbm, out_hbm,
+    q_ref, kv_ref, o_ref, bias_ref, len_ref,
+    load_sem, q_sem, len_sem, out_sem, send_sem, recv_sem,
 ):
     rows = q_ref.shape[0]
     reach = CYCLE * uly
-    routes, order = routes_for(uly, blocks)
+    routes, hops = routes_for(uly, blocks)
     period = len(routes)
     b = lax.axis_index("blk") * uly + lax.axis_index("uly")
     role = lax.rem(b, period)
@@ -60,12 +66,14 @@
         ]
 
     q_copy = pltpu.make_async_copy(q_hbm, q_ref, q_sem)
+    len_copy = pltpu.make_async_copy(len_hbm, len_ref, len_sem)
 
     @pl.loop(0, KEY_VALUE_HEADS)
     def _(g):
         for copy in loads(g):
             copy.start()
 
+    len_copy.start()
     q_copy.start()
 
     spans = sorted({abs(delta) for role_routes in routes for _, delta, _ in role_routes})
@@ -92,19 +100,12 @@
                     (2, rows, HEAD_SIZE), kv_ref.dtype
                 )
 
-    q_pos = b * rows + lax.broadcasted_iota(jnp.int32, (rows, 1), 0)
-    first = jnp.zeros((rows, 1), jnp.int32)
-    end = jnp.int32(0)
-    for d in range(len_ref.shape[0]):
-        end = end + len_ref[d]
-        first = jnp.where(q_pos >= end, end, first)
-    k_pos = (b - reach) * rows + lax.broadcasted_iota(jnp.int32, bias_ref.shape, 1)
-    bias_ref[...] = jnp.where((k_pos <= q_pos) & (k_pos >= first), 0.0, NEG_FILL)
-
     pl.semaphore_wait(barrier, expected)
 
-    def each_route(g, only, act):
+    def each_route(g, only, act, roles=None):
         for r, role_routes in enumerate(routes):
+            if roles is not None and r not in roles:
+                continue
             for n, (slot, delta, parity) in enumerate(role_routes):
                 if slot not in only:
                     continue
@@ -135,6 +136,16 @@
     def _(g):
         send_own(g)
 
+    len_copy.wait()
+    q_pos = b * rows + lax.broadcasted_iota(jnp.int32, (rows, 1), 0)
+    first = jnp.zeros((rows, 1), jnp.int32)
+    end = jnp.int32(0)
+    for d in range(len_ref.shape[0]):
+        end = end + len_ref[d]
+        first = jnp.where(q_pos >= end, end, first)
+    k_pos = (b - reach) * rows + lax.broadcasted_iota(jnp.int32, bias_ref.shape, 1)
+    bias_ref[...] = jnp.where((k_pos <= q_pos) & (k_pos >= first), 0.0, NEG_FILL)
+
     q_copy.wait()
     factor = math.log2(math.e) / math.sqrt(HEAD_SIZE)
 
@@ -143,22 +154,19 @@
         cols = pl.ds(pl.multiple_of(g * width, width), width)
         return pltpu.make_async_copy(o_ref.at[:, cols], out_hbm.at[:, cols], out_sem.at[g])
 
-    @pl.loop(0, KEY_VALUE_HEADS)
-    def _(g):
-        @pl.when(g + AHEAD < KEY_VALUE_HEADS)
-        def _():
-            send_own(g + AHEAD)
-
-        for slot in order:
-
-            @pl.when(b >= slot)
-            def _():
-                pltpu.make_async_copy(
-                    place(g, slot), place(g, slot), recv_sem.at[slot - 1, g]
-                ).wait()
-
-            each_route(g, (slot,), lambda copy: copy.start())
-
+    def receive(g, role_slots):
+        for r, slots in enumerate(role_slots):
+            for slot in slots:
+
+                @pl.when((role == r) & (b >= slot))
+                def _():
+                    pltpu.make_async_copy(
+                        place(g, slot), place(g, slot), recv_sem.at[slot - 1, g]
+                    ).wait()
+
+                each_route(g, (slot,), lambda copy: copy.start(), (r,))
+
+    def attend(g):
         keys = kv_ref[g, 0]
         values = kv_ref[g, 1]
 
@@ -183,6 +191,28 @@
             o_ref[:, cols(r)] = (summed[r * rows:(r + 1) * rows] / totals[r]).astype(o_ref.dtype)
         out_copy(g).start()
 
+    depth = max(len(stages) for stages in hops)
+    lag = sum(
+        jnp.where(role == r, max(h for h, slots in enumerate(stages) if slots), 0)
+        for r, stages in enumerate(hops)
+    )
+
+    @pl.loop(0, KEY_VALUE_HEADS + depth - 1)
+    def _(t):
+        @pl.when(t + AHEAD < KEY_VALUE_HEADS)
+        def _():
+            send_own(t + AHEAD)
+
+        for hop in range(depth):
+
+            @pl.when((t >= hop) & (t - hop < KEY_VALUE_HEADS))
+            def _():
+                receive(t - hop, [stages[hop] for stages in hops])
+
+        @pl.when((t >= lag) & (t - lag < KEY_VALUE_HEADS))
+        def _():
+            attend(t - lag)
+
     @pl.loop(0, KEY_VALUE_HEADS)
     def _(g):
         each_route(g, tuple(range(reach + 1)), lambda copy: copy.wait_send())
@@ -200,14 +230,16 @@
     return pl.pallas_call(
         functools.partial(kernel, uly, blocks),
         out_shape=jax.ShapeDtypeStruct(queries.shape, queries.dtype),
-        in_specs=[any_space, any_space, any_space, pl.BlockSpec(memory_space=pltpu.SMEM)],
+        in_specs=[any_space, any_space, any_space, any_space],
         out_specs=any_space,
         scratch_shapes=[
             pltpu.VMEM(queries.shape, queries.dtype),
             pltpu.VMEM((KEY_VALUE_HEADS, 2, span, HEAD_SIZE), keys.dtype),
             pltpu.VMEM(queries.shape, queries.dtype),
             pltpu.VMEM((rows, span), jnp.float32),
+            pltpu.SMEM(doc_lengths.shape, doc_lengths.dtype),
             pltpu.SemaphoreType.DMA((2, KEY_VALUE_HEADS)),
+            pltpu.SemaphoreType.DMA,
             pltpu.SemaphoreType.DMA,
             pltpu.SemaphoreType.DMA((KEY_VALUE_HEADS,)),
             pltpu.SemaphoreType.DMA((most, KEY_VALUE_HEADS)),
@@ -219,7 +251,7 @@
             transcendentals=rows * span * QUERY_HEADS,
         ),
         compiler_params=pltpu.CompilerParams(
-            collective_id=0, has_side_effects=True, vmem_limit_bytes=48 * 1024 * 1024
+            collective_id=0, has_side_effects=True, vmem_limit_bytes=60 * 1024 * 1024
         ),
     )(queries, keys, values, doc_lengths)
 

time: 42 us -> 28.8 us (0.69)
  the two profiles are of different devices: /device:TPU:16 before, /device:TPU:8 now
where the time goes in v2:
time: 28.8 us; the launch traced here: 28.4 us
  Pallas kernels  26.1 us (91%)
  local copies, waits for them, and re-layouts  2.29 us (8%)
    pallas_call x1, Pallas kernels, per_device(): pl.pallas_call(functools.partial(kernel, uly, blocks), out_shape=jax.Shap...  26.1 us
    unnamed x1, local copies, waits for them, and re-layouts  2.29 us

profile of v2, /device:TPU:8, one launch (start us, length us, event | category | flops | bytes accessed | tf_op | source)
XLA Modules:
  0.0 28.4 jit_solution(8070379158480558613)
XLA Ops:
  0.0 26.1 %shard_map.46 = bf16[128,4096]{1,0:T(8,128)(2,1)} custom-call(bf16[128,4096]{1,0:T(8,128)(2,1)} %q_hbm.1, bf16[128,1024]{1,0:T(8,128)(2,1)} %k_hbm.1, bf16[128,1024]{1,0:T(8,128)(2,1)} %v_hbm.1, s32[5]{0:T(128)} %len_hbm.1), custom_call_target="tpu_custom_call" | custom-call | flops 1342177280 | bytes 2621440 | tf_op jit(solution)/shard_map/pallas_call | solution.py:230
  26.1 2.3 %copy.6 = bf16[128,4096]{1,0:T(8,128)(2,1)} copy(bf16[128,4096]{1,0:T(8,128)(2,1)} %shard_map.46) | data formatting | bytes 2097152

commit v3 on v2

--- a/solution.py
+++ b/solution.py
@@ -15,7 +15,8 @@
 GROUP = QUERY_HEADS // KEY_VALUE_HEADS
 
 NEG_FILL = -1e30
-AHEAD = 3
+FAR_AHEAD = 5
+NEAR_AHEAD = 2
 
 FOUR = (
     ((0, 4, None), (0, 1, None), (0, 2, None)),
@@ -40,9 +41,9 @@
 
 
 def kernel(
-    uly, blocks, q_hbm, k_hbm, v_hbm, len_hbm, out_hbm,
-    q_ref, kv_ref, o_ref, bias_ref, len_ref,
-    load_sem, q_sem, len_sem, out_sem, send_sem, recv_sem,
+    uly, blocks, q_hbm, k_hbm, v_hbm, len_hbm, o_ref,
+    q_ref, kv_ref, bias_ref, len_ref,
+    load_sem, q_sem, len_sem, send_sem, recv_sem,
 ):
     rows = q_ref.shape[0]
     reach = CYCLE * uly
@@ -102,12 +103,12 @@
 
     pl.semaphore_wait(barrier, expected)
 
-    def each_route(g, only, act, roles=None):
+    def each_route(g, only, act, roles=None, far=None):
         for r, role_routes in enumerate(routes):
             if roles is not None and r not in roles:
                 continue
             for n, (slot, delta, parity) in enumerate(role_routes):
-                if slot not in only:
+                if slot not in only or (far is not None and far != (delta == reach)):
                     continue
                 other = b + delta
                 go = (role == r) & (b >= slot) & (other >= 0) & (other < blocks)
@@ -127,14 +128,21 @@
                         )
                     )
 
-    def send_own(g):
+    def send_far(g):
         for copy in loads(g):
             copy.wait()
-        each_route(g, (0,), lambda copy: copy.start())
-
-    @pl.loop(0, AHEAD)
+        each_route(g, (0,), lambda copy: copy.start(), far=True)
+
+    def send_near(g):
+        each_route(g, (0,), lambda copy: copy.start(), far=False)
+
+    @pl.loop(0, FAR_AHEAD)
     def _(g):
-        send_own(g)
+        send_far(g)
+
+        @pl.when(g < NEAR_AHEAD)
+        def _():
+            send_near(g)
 
     len_copy.wait()
     q_pos = b * rows + lax.broadcasted_iota(jnp.int32, (rows, 1), 0)
@@ -149,11 +157,6 @@
     q_copy.wait()
     factor = math.log2(math.e) / math.sqrt(HEAD_SIZE)
 
-    def out_copy(g):
-        width = GROUP * HEAD_SIZE
-        cols = pl.ds(pl.multiple_of(g * width, width), width)
-        return pltpu.make_async_copy(o_ref.at[:, cols], out_hbm.at[:, cols], out_sem.at[g])
-
     def receive(g, role_slots):
         for r, slots in enumerate(role_slots):
             for slot in slots:
@@ -177,19 +180,19 @@
         scores = lax.dot_general(
             queries, keys, (((1,), (1,)), ((), ())), preferred_element_type=jnp.float32
         )
-        parts, totals = [], []
+        parts = []
         for r in range(GROUP):
             part = scores[r * rows:(r + 1) * rows] + bias_ref[...]
             peak = jnp.max(part, axis=1, keepdims=True)
-            weights = jnp.exp2((part - peak) * factor)
-            totals.append(jnp.sum(weights, axis=1, keepdims=True))
-            parts.append(weights.astype(jnp.bfloat16))
+            parts.append(jnp.exp2((part - peak) * factor).astype(jnp.bfloat16))
         summed = jnp.dot(
-            jnp.concatenate(parts, axis=0), values, preferred_element_type=jnp.float32
+            jnp.concatenate(parts, axis=0),
+            jnp.concatenate([values, jnp.ones_like(values)], axis=1),
+            preferred_element_type=jnp.float32,
         )
+        result = (summed[:, :HEAD_SIZE] / summed[:, HEAD_SIZE:]).astype(o_ref.dtype)
         for r in range(GROUP):
-            o_ref[:, cols(r)] = (summed[r * rows:(r + 1) * rows] / totals[r]).astype(o_ref.dtype)
-        out_copy(g).start()
+            o_ref[:, cols(r)] = result[r * rows:(r + 1) * rows]
 
     depth = max(len(stages) for stages in hops)
     lag = sum(
@@ -199,9 +202,13 @@
 
     @pl.loop(0, KEY_VALUE_HEADS + depth - 1)
     def _(t):
-        @pl.when(t + AHEAD < KEY_VALUE_HEADS)
-        def _():
-            send_own(t + AHEAD)
+        @pl.when(t + FAR_AHEAD < KEY_VALUE_HEADS)
+        def _():
+            send_far(t + FAR_AHEAD)
+
+        @pl.when(t + NEAR_AHEAD < KEY_VALUE_HEADS)
+        def _():
+            send_near(t + NEAR_AHEAD)
 
         for hop in range(depth):
 
@@ -216,7 +223,6 @@
     @pl.loop(0, KEY_VALUE_HEADS)
     def _(g):
         each_route(g, tuple(range(reach + 1)), lambda copy: copy.wait_send())
-        out_copy(g).wait()
 
 
 def per_device(uly, blocks, queries, keys, values, doc_lengths):
@@ -226,22 +232,19 @@
     most = max(len(role_routes) for role_routes in routes)
     span = (reach + 1) * rows
     flops = 4 * rows * span * QUERY_HEADS * HEAD_SIZE
-    any_space = pl.BlockSpec(memory_space=pl.ANY)
     return pl.pallas_call(
         functools.partial(kernel, uly, blocks),
-        out_shape=jax.ShapeDtypeStruct(queries.shape, queries.dtype),
-        in_specs=[any_space, any_space, any_space, any_space],
-        out_specs=any_space,
+        out_shape=pltpu.VMEM(queries.shape, queries.dtype),
+        in_specs=[pl.BlockSpec(memory_space=pl.ANY)] * 4,
+        out_specs=pl.BlockSpec(memory_space=pltpu.VMEM),
         scratch_shapes=[
             pltpu.VMEM(queries.shape, queries.dtype),
             pltpu.VMEM((KEY_VALUE_HEADS, 2, span, HEAD_SIZE), keys.dtype),
-            pltpu.VMEM(queries.shape, queries.dtype),
             pltpu.VMEM((rows, span), jnp.float32),
             pltpu.SMEM(doc_lengths.shape, doc_lengths.dtype),
             pltpu.SemaphoreType.DMA((2, KEY_VALUE_HEADS)),
             pltpu.SemaphoreType.DMA,
             pltpu.SemaphoreType.DMA,
-            pltpu.SemaphoreType.DMA((KEY_VALUE_HEADS,)),
             pltpu.SemaphoreType.DMA((most, KEY_VALUE_HEADS)),
             pltpu.SemaphoreType.DMA((reach, KEY_VALUE_HEADS)),
         ],

time: 28.8 us -> 31.8 us (1.10)
  Pallas kernels: 26.1 us -> 30.3 us
  local copies, waits for them, and re-layouts: 2.29 us -> 0.97 us
    pallas_call x1, Pallas kernels: 26.1 us -> 30.3 us  [per_device(): pl.pallas_call(functools.partial(kernel, uly, blocks), out_shape=pltpu.VM...]
    unnamed x1, local copies, waits for them, and re-layouts: 2.29 us -> 0.97 us
where the time goes in v3:
time: 31.8 us; the launch traced here: 31.2 us
  Pallas kernels  30.3 us (95%)
  local copies, waits for them, and re-layouts  0.97 us (3%)
    pallas_call x1, Pallas kernels, per_device(): pl.pallas_call(functools.partial(kernel, uly, blocks), out_shape=pltpu.VM...  30.3 us
    unnamed x1, local copies, waits for them, and re-layouts  0.97 us

profile of v3, /device:TPU:8, one launch (start us, length us, event | category | flops | bytes accessed | tf_op | source)
XLA Modules:
  0.0 31.2 jit_solution(11474079206945566465)
XLA Ops:
  0.0 30.3 %shard_map.46 = bf16[128,4096]{1,0:T(8,128)(2,1)S(1)} custom-call(bf16[128,4096]{1,0:T(8,128)(2,1)} %q_hbm.1, bf16[128,1024]{1,0:T(8,128)(2,1)} %k_hbm.1, bf16[128,1024]{1,0:T(8,128)(2,1)} %v_hbm.1, s32[5]{0:T(128)} %len_hbm.1), custom_call_target="tpu_custom_call" | custom-call | flops 1342177280 | bytes 2621440 | tf_op jit(solution)/shard_map/pallas_call | solution.py:235
  30.3 1.0 %copy.6 = bf16[128,4096]{1,0:T(8,128)(2,1)} copy(bf16[128,4096]{1,0:T(8,128)(2,1)S(1)} %shard_map.46) | data formatting | bytes 2097152

commit v4 on v3

--- a/solution.py
+++ b/solution.py
@@ -15,7 +15,7 @@
 GROUP = QUERY_HEADS // KEY_VALUE_HEADS
 
 NEG_FILL = -1e30
-FAR_AHEAD = 5
+FAR_AHEAD = (1, 2, 3, 4)
 NEAR_AHEAD = 2
 
 FOUR = (
@@ -25,10 +25,10 @@
     ((0, 4, None), (1, 2, 0), (4, -1, None), (4, -2, None)),
 )
 FOUR_HOPS = (
-    ((4,), (2, 3), (1,)),
+    ((), (), (4, 2, 3, 1)),
     ((4, 1), (2, 3), ()),
-    ((4, 1, 2), (3,), ()),
-    ((4, 1, 2), (3,), ()),
+    ((4, 1), (2, 3), ()),
+    ((4, 1), (2, 3), ()),
 )
 
 
@@ -128,17 +128,24 @@
                         )
                     )
 
-    def send_far(g):
+    @pl.loop(0, KEY_VALUE_HEADS)
+    def _(g):
         for copy in loads(g):
             copy.wait()
+
+    def send_far(g):
         each_route(g, (0,), lambda copy: copy.start(), far=True)
 
     def send_near(g):
         each_route(g, (0,), lambda copy: copy.start(), far=False)
 
-    @pl.loop(0, FAR_AHEAD)
-    def _(g):
-        send_far(g)
+    far_ahead = sum(jnp.where(role == r, FAR_AHEAD[r], 0) for r in range(period))
+
+    @pl.loop(0, max(NEAR_AHEAD, *FAR_AHEAD))
+    def _(g):
+        @pl.when(g < far_ahead)
+        def _():
+            send_far(g)
 
         @pl.when(g < NEAR_AHEAD)
         def _():
@@ -202,9 +209,9 @@
 
     @pl.loop(0, KEY_VALUE_HEADS + depth - 1)
     def _(t):
-        @pl.when(t + FAR_AHEAD < KEY_VALUE_HEADS)
-        def _():
-            send_far(t + FAR_AHEAD)
+        @pl.when(t + far_ahead < KEY_VALUE_HEADS)
+        def _():
+            send_far(t + far_ahead)
 
         @pl.when(t + NEAR_AHEAD < KEY_VALUE_HEADS)
         def _():

time: 31.8 us -> 28.8 us (0.906); the launches traced: 31.2 us -> 28.7 us
  Pallas kernels: 30.3 us -> 27.7 us
    pallas_call x1, Pallas kernels: 30.3 us -> 27.7 us  [per_device(): pl.pallas_call(functools.partial(kernel, uly, blocks), out_shape=pltpu.VM...]
where the time goes in v4:
time: 28.8 us; the launch traced here: 28.7 us
  Pallas kernels  27.7 us (96%)
  local copies, waits for them, and re-layouts  0.97 us (3%)
    pallas_call x1, Pallas kernels, per_device(): pl.pallas_call(functools.partial(kernel, uly, blocks), out_shape=pltpu.VM...  27.7 us
    unnamed x1, local copies, waits for them, and re-layouts  0.97 us

profile of v4, /device:TPU:8, one launch (start us, length us, event | category | flops | bytes accessed | tf_op | source)
XLA Modules:
  0.0 28.7 jit_solution(2967095879113249578)
XLA Ops:
  0.0 27.7 %shard_map.46 = bf16[128,4096]{1,0:T(8,128)(2,1)S(1)} custom-call(bf16[128,4096]{1,0:T(8,128)(2,1)} %q_hbm.1, bf16[128,1024]{1,0:T(8,128)(2,1)} %k_hbm.1, bf16[128,1024]{1,0:T(8,128)(2,1)} %v_hbm.1, s32[5]{0:T(128)} %len_hbm.1), custom_call_target="tpu_custom_call" | custom-call | flops 1342177280 | bytes 2621440 | tf_op jit(solution)/shard_map/pallas_call | solution.py:242
  27.7 1.0 %copy.6 = bf16[128,4096]{1,0:T(8,128)(2,1)} copy(bf16[128,4096]{1,0:T(8,128)(2,1)S(1)} %shard_map.46) | data formatting | bytes 2097152

commit v5 on v3

--- a/solution.py
+++ b/solution.py
@@ -15,8 +15,7 @@
 GROUP = QUERY_HEADS // KEY_VALUE_HEADS
 
 NEG_FILL = -1e30
-FAR_AHEAD = 5
-NEAR_AHEAD = 2
+AHEAD = 3
 
 FOUR = (
     ((0, 4, None), (0, 1, None), (0, 2, None)),
@@ -103,46 +102,58 @@
 
     pl.semaphore_wait(barrier, expected)
 
-    def each_route(g, only, act, roles=None, far=None):
-        for r, role_routes in enumerate(routes):
-            if roles is not None and r not in roles:
+    def start(r, g, from_slot):
+        for n, (slot, delta, parity) in enumerate(routes[r]):
+            if slot != from_slot:
                 continue
-            for n, (slot, delta, parity) in enumerate(role_routes):
-                if slot not in only or (far is not None and far != (delta == reach)):
-                    continue
-                other = b + delta
-                go = (role == r) & (b >= slot) & (other >= 0) & (other < blocks)
-                if parity is not None:
-                    go = go & (lax.rem(g, 2) == parity)
-
-                @pl.when(go)
-                def _():
-                    act(
-                        pltpu.make_async_remote_copy(
-                            src_ref=place(g, slot),
-                            dst_ref=place(g, slot + delta),
-                            send_sem=send_sem.at[n, g],
-                            recv_sem=recv_sem.at[slot + delta - 1, g],
-                            device_id=target(other),
-                            device_id_type=pl.DeviceIdType.MESH,
-                        )
-                    )
-
-    def send_far(g):
+            other = b + delta
+            go = (other >= 0) & (other < blocks)
+            if parity is not None:
+                go = go & (lax.rem(g, 2) == parity)
+
+            @pl.when(go)
+            def _():
+                pltpu.make_async_remote_copy(
+                    src_ref=place(g, slot),
+                    dst_ref=place(g, slot + delta),
+                    send_sem=send_sem.at[n],
+                    recv_sem=recv_sem.at[slot + delta - 1, g],
+                    device_id=target(other),
+                    device_id_type=pl.DeviceIdType.MESH,
+                ).start()
+
+    def receive(r, g, slots):
+        for slot in slots:
+
+            @pl.when(b >= slot)
+            def _():
+                pltpu.make_async_copy(
+                    place(g, slot), place(g, slot), recv_sem.at[slot - 1, g]
+                ).wait()
+                start(r, g, slot)
+
+    def all_sent(r):
+        for n, (slot, delta, parity) in enumerate(routes[r]):
+            other = b + delta
+            heads = KEY_VALUE_HEADS if parity is None else KEY_VALUE_HEADS // 2
+
+            @pl.when((b >= slot) & (other >= 0) & (other < blocks))
+            def _():
+                sent = kv_ref.at[pl.ds(0, heads), :, pl.ds((reach - slot) * rows, rows), :]
+                pltpu.make_async_copy(sent, sent, send_sem.at[n]).wait()
+
+    @pl.loop(0, KEY_VALUE_HEADS)
+    def _(g):
         for copy in loads(g):
             copy.wait()
-        each_route(g, (0,), lambda copy: copy.start(), far=True)
-
-    def send_near(g):
-        each_route(g, (0,), lambda copy: copy.start(), far=False)
-
-    @pl.loop(0, FAR_AHEAD)
-    def _(g):
-        send_far(g)
-
-        @pl.when(g < NEAR_AHEAD)
-        def _():
-            send_near(g)
+
+    for r in range(period):
+
+        @pl.when(role == r)
+        def _():
+            @pl.loop(0, AHEAD)
+            def _(g):
+                start(r, g, 0)
 
     len_copy.wait()
     q_pos = b * rows + lax.broadcasted_iota(jnp.int32, (rows, 1), 0)
@@ -156,18 +167,6 @@
 
     q_copy.wait()
     factor = math.log2(math.e) / math.sqrt(HEAD_SIZE)
-
-    def receive(g, role_slots):
-        for r, slots in enumerate(role_slots):
-            for slot in slots:
-
-                @pl.when((role == r) & (b >= slot))
-                def _():
-                    pltpu.make_async_copy(
-                        place(g, slot), place(g, slot), recv_sem.at[slot - 1, g]
-                    ).wait()
-
-                each_route(g, (slot,), lambda copy: copy.start(), (r,))
 
     def attend(g):
         keys = kv_ref[g, 0]
@@ -202,27 +201,30 @@
 
     @pl.loop(0, KEY_VALUE_HEADS + depth - 1)
     def _(t):
-        @pl.when(t + FAR_AHEAD < KEY_VALUE_HEADS)
-        def _():
-            send_far(t + FAR_AHEAD)
-
-        @pl.when(t + NEAR_AHEAD < KEY_VALUE_HEADS)
-        def _():
-            send_near(t + NEAR_AHEAD)
-
-        for hop in range(depth):
-
-            @pl.when((t >= hop) & (t - hop < KEY_VALUE_HEADS))
-            def _():
-                receive(t - hop, [stages[hop] for stages in hops])
+        for r, stages in enumerate(hops):
+
+            @pl.when(role == r)
+            def _():
+                @pl.when(t + AHEAD < KEY_VALUE_HEADS)
+                def _():
+                    start(r, t + AHEAD, 0)
+
+                for hop, slots in enumerate(stages):
+                    if slots:
+
+                        @pl.when((t >= hop) & (t - hop < KEY_VALUE_HEADS))
+                        def _():
+                            receive(r, t - hop, slots)
 
         @pl.when((t >= lag) & (t - lag < KEY_VALUE_HEADS))
         def _():
             attend(t - lag)
 
-    @pl.loop(0, KEY_VALUE_HEADS)
-    def _(g):
-        each_route(g, tuple(range(reach + 1)), lambda copy: copy.wait_send())
+    for r in range(period):
+
+        @pl.when(role == r)
+        def _():
+            all_sent(r)
 
 
 def per_device(uly, blocks, queries, keys, values, doc_lengths):
@@ -245,7 +247,7 @@
             pltpu.SemaphoreType.DMA((2, KEY_VALUE_HEADS)),
             pltpu.SemaphoreType.DMA,
             pltpu.SemaphoreType.DMA,
-            pltpu.SemaphoreType.DMA((most, KEY_VALUE_HEADS)),
+            pltpu.SemaphoreType.DMA((most,)),
             pltpu.SemaphoreType.DMA((reach, KEY_VALUE_HEADS)),
         ],
         cost_estimate=pl.CostEstimate(

time: 31.8 us -> 26.9 us (0.85)
  Pallas kernels: 30.3 us -> 25.4 us
    pallas_call x1, Pallas kernels: 30.3 us -> 25.4 us  [per_device(): pl.pallas_call(functools.partial(kernel, uly, blocks), out_shape=pltpu.VM...]
where the time goes in v5:
time: 26.9 us; the launch traced here: 26.4 us
  Pallas kernels  25.4 us (94%)
  local copies, waits for them, and re-layouts  0.97 us (4%)
    pallas_call x1, Pallas kernels, per_device(): pl.pallas_call(functools.partial(kernel, uly, blocks), out_shape=pltpu.VM...  25.4 us
    unnamed x1, local copies, waits for them, and re-layouts  0.97 us

profile of v5, /device:TPU:8, one launch (start us, length us, event | category | flops | bytes accessed | tf_op | source)
XLA Modules:
  0.0 26.4 jit_solution(4750134149470717960)
XLA Ops:
  0.0 25.4 %shard_map.46 = bf16[128,4096]{1,0:T(8,128)(2,1)S(1)} custom-call(bf16[128,4096]{1,0:T(8,128)(2,1)} %q_hbm.1, bf16[128,1024]{1,0:T(8,128)(2,1)} %k_hbm.1, bf16[128,1024]{1,0:T(8,128)(2,1)} %v_hbm.1, s32[5]{0:T(128)} %len_hbm.1), custom_call_target="tpu_custom_call" | custom-call | flops 1342177280 | bytes 2621440 | tf_op jit(solution)/shard_map/pallas_call | solution.py:237
  25.4 1.0 %copy.6 = bf16[128,4096]{1,0:T(8,128)(2,1)} copy(bf16[128,4096]{1,0:T(8,128)(2,1)S(1)} %shard_map.46) | data formatting | bytes 2097152

commit v6 on v5

--- a/solution.py
+++ b/solution.py
@@ -15,7 +15,7 @@
 GROUP = QUERY_HEADS // KEY_VALUE_HEADS
 
 NEG_FILL = -1e30
-AHEAD = 3
+AHEAD = 2
 
 FOUR = (
     ((0, 4, None), (0, 1, None), (0, 2, None)),

time: 26.9 us -> 26.6 us (0.989); the launches traced: 26.4 us -> 26.4 us
  no operation moved by 1% of the time
where the time goes in v6:
time: 26.6 us; the launch traced here: 26.4 us
  Pallas kernels  25.4 us (95%)
  local copies, waits for them, and re-layouts  0.97 us (4%)
    pallas_call x1, Pallas kernels, per_device(): pl.pallas_call(functools.partial(kernel, uly, blocks), out_shape=pltpu.VM...  25.4 us
    unnamed x1, local copies, waits for them, and re-layouts  0.97 us

profile of v6, /device:TPU:8, one launch (start us, length us, event | category | flops | bytes accessed | tf_op | source)
XLA Modules:
  0.0 26.4 jit_solution(9797331326631669605)
XLA Ops:
  0.0 25.4 %shard_map.46 = bf16[128,4096]{1,0:T(8,128)(2,1)S(1)} custom-call(bf16[128,4096]{1,0:T(8,128)(2,1)} %q_hbm.1, bf16[128,1024]{1,0:T(8,128)(2,1)} %k_hbm.1, bf16[128,1024]{1,0:T(8,128)(2,1)} %v_hbm.1, s32[5]{0:T(128)} %len_hbm.1), custom_call_target="tpu_custom_call" | custom-call | flops 1342177280 | bytes 2621440 | tf_op jit(solution)/shard_map/pallas_call | solution.py:237
  25.4 1.0 %copy.6 = bf16[128,4096]{1,0:T(8,128)(2,1)} copy(bf16[128,4096]{1,0:T(8,128)(2,1)S(1)} %shard_map.46) | data formatting | bytes 2097152

commit v7 on v6

--- a/solution.py
+++ b/solution.py
@@ -18,9 +18,9 @@
 AHEAD = 2
 
 FOUR = (
-    ((0, 4, None), (0, 1, None), (0, 2, None)),
-    ((0, 4, None), (0, 1, None), (0, 2, None), (1, 2, None), (4, -1, 1)),
-    ((0, 4, None), (0, 1, None), (1, 2, 0), (4, -2, None), (4, -1, 1), (3, -2, None)),
+    ((0, 1, None), (0, 4, None), (0, 2, None)),
+    ((0, 1, None), (0, 4, None), (0, 2, None), (1, 2, None), (4, -1, 1)),
+    ((0, 1, None), (0, 4, None), (1, 2, 0), (4, -2, None), (4, -1, 1), (3, -2, None)),
     ((0, 4, None), (1, 2, 0), (4, -1, None), (4, -2, None)),
 )
 FOUR_HOPS = (

time: 26.6 us -> 26.6 us (level)
  no operation moved by 1% of the time
where the time goes in v7:
time: 26.6 us; the launch traced here: 26.4 us
  Pallas kernels  25.4 us (95%)
  local copies, waits for them, and re-layouts  0.97 us (4%)
    pallas_call x1, Pallas kernels, per_device(): pl.pallas_call(functools.partial(kernel, uly, blocks), out_shape=pltpu.VM...  25.4 us
    unnamed x1, local copies, waits for them, and re-layouts  0.97 us

profile of v7, /device:TPU:8, one launch (start us, length us, event | category | flops | bytes accessed | tf_op | source)
XLA Modules:
  0.0 26.4 jit_solution(2110554387277035074)
XLA Ops:
  0.0 25.4 %shard_map.46 = bf16[128,4096]{1,0:T(8,128)(2,1)S(1)} custom-call(bf16[128,4096]{1,0:T(8,128)(2,1)} %q_hbm.1, bf16[128,1024]{1,0:T(8,128)(2,1)} %k_hbm.1, bf16[128,1024]{1,0:T(8,128)(2,1)} %v_hbm.1, s32[5]{0:T(128)} %len_hbm.1), custom_call_target="tpu_custom_call" | custom-call | flops 1342177280 | bytes 2621440 | tf_op jit(solution)/shard_map/pallas_call | solution.py:237
  25.4 1.0 %copy.6 = bf16[128,4096]{1,0:T(8,128)(2,1)} copy(bf16[128,4096]{1,0:T(8,128)(2,1)S(1)} %shard_map.46) | data formatting | bytes 2097152

commit v8 on v7

--- a/solution.py
+++ b/solution.py
@@ -24,7 +24,7 @@
     ((0, 4, None), (1, 2, 0), (4, -1, None), (4, -2, None)),
 )
 FOUR_HOPS = (
-    ((4,), (2, 3), (1,)),
+    ((), (), (4, 2, 3, 1)),
     ((4, 1), (2, 3), ()),
     ((4, 1, 2), (3,), ()),
     ((4, 1, 2), (3,), ()),

time: 26.6 us -> 25.4 us (0.955)
  Pallas kernels: 25.4 us -> 24.3 us
    pallas_call x1, Pallas kernels: 25.4 us -> 24.3 us  [per_device(): pl.pallas_call(functools.partial(kernel, uly, blocks), out_shape=pltpu.VM...]
where the time goes in v8:
time: 25.4 us; the launch traced here: 25.3 us
  Pallas kernels  24.3 us (96%)
  local copies, waits for them, and re-layouts  0.97 us (4%)
    pallas_call x1, Pallas kernels, per_device(): pl.pallas_call(functools.partial(kernel, uly, blocks), out_shape=pltpu.VM...  24.3 us
    unnamed x1, local copies, waits for them, and re-layouts  0.97 us

profile of v8, /device:TPU:8, one launch (start us, length us, event | category | flops | bytes accessed | tf_op | source)
XLA Modules:
  0.0 25.3 jit_solution(7265567799353369966)
XLA Ops:
  0.0 24.3 %shard_map.46 = bf16[128,4096]{1,0:T(8,128)(2,1)S(1)} custom-call(bf16[128,4096]{1,0:T(8,128)(2,1)} %q_hbm.1, bf16[128,1024]{1,0:T(8,128)(2,1)} %k_hbm.1, bf16[128,1024]{1,0:T(8,128)(2,1)} %v_hbm.1, s32[5]{0:T(128)} %len_hbm.1), custom_call_target="tpu_custom_call" | custom-call | flops 1342177280 | bytes 2621440 | tf_op jit(solution)/shard_map/pallas_call | solution.py:237
  24.3 1.0 %copy.6 = bf16[128,4096]{1,0:T(8,128)(2,1)} copy(bf16[128,4096]{1,0:T(8,128)(2,1)S(1)} %shard_map.46) | data formatting | bytes 2097152
